TPU v7x, 128 devices: a whole 4x4x4 slice. The times are simulated.
128 devices in a mesh: gx: 16 (over x, z), gy: 8 (over y, core).
Axes of the slice: x: 4, y: 4, z: 4, core: 2. Of those that a mesh axis runs over, the one named last changes fastest.
Arguments:
- particle_pos: float32 [3, 2097152], P(None, ('gx', 'gy')), may hold values from 0 to 16
- tile_dest: int32 [16384, 1], P(('gx', 'gy')), may hold values from 0 to 127; in each aligned block of 128 rows (0 to 127, 128 to 255, ...) at most 2 rows name the same one
- tile_block: int32 [16384], P(('gx', 'gy')), may hold values from 0 to 127
- fluid_flag: int32 [512, 512, 256], P('gx', 'gy'), may hold values 0 or 1
- divergence: float32 [512, 512, 256], P('gx', 'gy'), may hold values from -6 to 6
Outputs:
- level_set: float32 [512, 512, 256], P('gx', 'gy')
- pressure: float32 [512, 512, 256], P('gx', 'gy')
Inputs may be any that keep to these rules, and one draw needn't show every extreme that they name: `tile_dest`: among the tiles of one device, no brick is named more than 2 times, a bound that some block reaches.
All inputs are finite; a program needn't handle non-finite values. No bound on the sum of `fluid_flag` on one device may be relied on, other than what follows from the above.
Results may differ from a plain program's by a relative error of at most 0.00002.
Values sent between devices are 32-bit elements; how exact they have to be, the bound alone decides.
No kernel may reach another device: no remote copies, remote signals or barrier semaphores. Data moves between devices by JAX's collectives and lax.ppermute only.
A program may use at most 128 MiB of HBM per device.

v0:
```python
import functools

import jax
import jax.numpy as jnp
from jax import lax
from jax.experimental import pallas as pl
from jax.experimental.pallas import tpu as pltpu
from jax.sharding import PartitionSpec as P

BLOCK = 16
TILE = 128
RADIUS = 1.2
BAND = 3.0
WEIGHT = 2.0 / 3.0
FAR = 1.0e9
HALO = 4
ROWS = 8
REACH = RADIUS + BAND + 1.0e-3
PAIRS = 8

f32 = jnp.float32


def ordered(keys, first, second):
    row = lax.broadcasted_iota(jnp.int32, (8, TILE), 0)
    data = [list(keys), list(first), list(second)]
    size = 2
    while size <= TILE:
        if size >= 16 and size < TILE:
            sign = jnp.where((row & (size // 16)) == 0, 1.0, -1.0).astype(f32)
        else:
            sign = None
        gap = size // 2
        while gap >= 1:
            if gap < 16:
                for v in range(16):
                    if v & gap:
                        continue
                    w = v | gap
                    a, b = data[0][v], data[0][w]
                    if sign is not None:
                        swap_now = a * sign > b * sign
                    elif size < 16 and v & size:
                        swap_now = a < b
                    else:
                        swap_now = a > b
                    for part in data:
                        a, b = part[v], part[w]
                        part[v] = jnp.where(swap_now, b, a)
                        part[w] = jnp.where(swap_now, a, b)
            else:
                e = gap // 16
                low = (row & e) == 0
                way = jnp.where(low, 1.0, -1.0).astype(f32)
                if sign is not None:
                    way = way * sign
                for v in range(16):
                    others = []
                    for part in data:
                        if e == 4:
                            others.append(pltpu.roll(part[v], 4, 0))
                        else:
                            others.append(jnp.where(low, pltpu.roll(part[v], 8 - e, 0), pltpu.roll(part[v], e, 0)))
                    take = data[0][v] * way > others[0] * way
                    for part, other in zip(data, others):
                        part[v] = jnp.where(take, other, part[v])
            gap //= 2
        size *= 2
    return data


def strip_copies(kind_in, div_in, first_ref, second_ref, kx_ref, ky_ref, dy_ref, sem):
    nx, ny, nz = kind_in.shape
    copies = []
    side = lax.axis_index("gx") % 2
    for n, (at, out) in enumerate((((1 - side) * (nx - HALO), first_ref), (side * (nx - HALO), second_ref))):
        planes = pl.ds(at, HALO)
        copies.append(pltpu.make_async_copy(kind_in.at[planes], kx_ref.at[n], sem.at[n]))
        copies.append(pltpu.make_async_copy(div_in.at[planes], out.at[1], sem.at[2 + n]))
    for n, at in enumerate((0, ny - 8)):
        rows = pl.ds(at, 8)
        copies.append(pltpu.make_async_copy(kind_in.at[:, rows, :], ky_ref.at[n], sem.at[4 + n]))
        copies.append(pltpu.make_async_copy(div_in.at[:, rows, :], dy_ref.at[n], sem.at[6 + n]))
    return copies


def cut_strips(first_ref, second_ref, face1_ref, face2_ref, kx_ref, ky_ref, dy_ref):
    first_ref[0] = kind_of(kx_ref[0])
    second_ref[0] = kind_of(kx_ref[1])
    low = slice(0, HALO)
    high = slice(8 - HALO, 8)
    even = lax.axis_index("gy") % 2 == 0
    for turn, out in ((True, face1_ref), (False, face2_ref)):
        up = even if turn else jnp.logical_not(even)
        out[0] = jnp.where(up, kind_of(ky_ref[1, :, high, :]), kind_of(ky_ref[0, :, low, :]))
        out[1] = jnp.where(up, dy_ref[1, :, high, :], dy_ref[0, :, low, :])


def pack_kernel(dest_in, block_in, pos_in, kind_in, div_in, send_ref, first_ref, second_ref, face1_ref, face2_ref,
                dest_ref, block_ref, pos_ref, count_ref, tile_ref, turn_ref, kx_ref, ky_ref, dy_ref, sem, strip_sem):
    tiles = block_ref.shape[0]
    copies = [
        pltpu.make_async_copy(a, b, sem.at[n])
        for n, (a, b) in enumerate(((pos_in, pos_ref), (dest_in, dest_ref), (block_in, block_ref)))
    ]
    strips = strip_copies(kind_in, div_in, first_ref, second_ref, kx_ref, ky_ref, dy_ref, strip_sem)
    for copy in copies + strips:
        copy.start()
    lane = lax.broadcasted_iota(jnp.int32, (4, TILE), 1)
    note = (lax.broadcasted_iota(jnp.int32, (4, TILE), 0) == 3) & (lane == 0)

    def clear(i, carry):
        count_ref[i] = 0
        return carry

    lax.fori_loop(0, count_ref.shape[0], clear, 0, unroll=16)
    empty = jnp.where(lane == 0, -1.0, 0.0).astype(f32)
    send_ref[...] = jnp.broadcast_to(empty[None], send_ref.shape)

    copies[0].wait()
    for t in range(tiles):
        tile_ref[0:3, t, :] = pos_ref[:, t * TILE : t * TILE + TILE]
    parts = []
    for c in range(3):
        turned = jnp.transpose(tile_ref[c], (1, 0))
        parts.append([turned[v * 8 : v * 8 + 8, :] for v in range(16)])
    parts = ordered(*parts)
    turn_ref[3] = jnp.zeros((TILE + 16, TILE), f32)
    for k in range(PAIRS):
        below = jnp.zeros((8, TILE), f32)
        upto = jnp.zeros((8, TILE), f32)
        for v in range(16):
            below = below + jnp.where(parts[0][v] < 2 * k + 0.5 - REACH, 1.0, 0.0)
            upto = upto + jnp.where(parts[0][v] < 2 * k + 1.5 + REACH, 1.0, 0.0)
        turn_ref[3, 1 + k : 2 + k, :] = jnp.sum(below, axis=0, keepdims=True) - TILE
        turn_ref[3, 1 + PAIRS + k : 2 + PAIRS + k, :] = -jnp.sum(upto, axis=0, keepdims=True)
    for c in range(3):
        for v in range(16):
            turn_ref[c, pl.ds(v, 8, stride=16), :] = parts[c][v]
    for c in range(4):
        tile_ref[c] = jnp.transpose(turn_ref[c, 0:TILE, :], (1, 0))

    for copy in copies[1:] + strips:
        copy.wait()
    cut_strips(first_ref, second_ref, face1_ref, face2_ref, kx_ref, ky_ref, dy_ref)

    def place(t, carry):
        owner = dest_ref[t]
        slot = count_ref[owner]
        count_ref[owner] = slot + 1
        send_ref[owner * 2 + slot] = jnp.where(note, block_ref[t].astype(f32), tile_ref[:, t, :])
        return carry

    lax.fori_loop(0, tiles, place, 0, unroll=16)


def ones_where(condition):
    return jnp.where(condition, 1.0, 0.0).astype(jnp.bfloat16)


def row_to_column(row):
    return jnp.concatenate(
        [
            jnp.transpose(jnp.broadcast_to(row[:, h : h + 128], (128, 128)), (1, 0))
            for h in range(0, row.shape[1], 128)
        ],
        axis=0,
    )


def arrange(notes, note_ref, slot_ref):
    records = notes.shape[0]
    halves = records // 128
    turned = [jnp.transpose(notes[h * 128 : h * 128 + 128, :], (1, 0)) for h in range(halves)]
    labels = jnp.concatenate([v[0:1, :] for v in turned], axis=1)
    shift = [v[1 : 1 + PAIRS] - v[1 + PAIRS : 1 + 2 * PAIRS] for v in turned]
    keys = jnp.concatenate([jnp.sum(v, axis=0, keepdims=True) for v in shift], axis=1)
    valid = labels >= 0.0
    spot = (labels.astype(jnp.int32) & 7).astype(f32)
    column = lax.broadcasted_iota(jnp.int32, (8, records), 0).astype(f32)
    member = jnp.where(valid & (column == spot), 1.0, 0.0)
    from_index = lax.broadcasted_iota(jnp.int32, (records, records), 0)
    to_index = lax.broadcasted_iota(jnp.int32, (records, records), 1)
    earlier = ones_where(from_index < to_index)
    own = row_to_column(keys)
    own = jnp.concatenate([own] * halves, axis=1)
    smaller = (own < keys) | ((own == keys) & (from_index < to_index))
    before = jnp.dot(member.astype(jnp.bfloat16), ones_where(smaller), preferred_element_type=f32)
    rank = jnp.sum(member * before, axis=0, keepdims=True)
    counts = jnp.sum(member, axis=1, keepdims=True)
    total = jnp.sum(counts, axis=0, keepdims=True)
    room = 8.0 * jnp.floor((total + 63.0) * (1.0 / 64.0))
    late = jnp.where(valid & (rank >= room), 1.0, 0.0)
    turn = jnp.dot(jnp.broadcast_to(late, (8, records)).astype(jnp.bfloat16), earlier, preferred_element_type=f32)[0:1]
    used = jnp.minimum(counts, room)
    free = room - used
    offsets = [jnp.zeros((1, 1), f32)]
    for t in range(7):
        offsets.append(offsets[-1] + free[t : t + 1])
    offset = jnp.concatenate(offsets, axis=0)
    chosen = (turn >= offset) & (turn < offset + free)
    moved = jnp.sum(jnp.where(chosen, (used + turn - offset) * 8.0 + column, 0.0), axis=0, keepdims=True)
    slots = jnp.where(valid, jnp.where(late > 0.0, moved, rank * 8.0 + spot), -1.0)
    slot_ref[...] = slots
    lane = lax.broadcasted_iota(jnp.int32, (records, 128), 1).astype(f32)
    raised = jnp.broadcast_to(jnp.where(valid, labels + 1.0, 0.0), (8, records)).astype(jnp.bfloat16)
    late_slots = jnp.broadcast_to(jnp.where(late > 0.0, slots + 1.0, 0.0), (8, records)).astype(jnp.bfloat16)
    to_slot = row_to_column(slots)
    to_turn = row_to_column(jnp.where(late > 0.0, turn, -1.0))
    for h in range(halves):
        here = jnp.dot(raised, ones_where(to_slot == lane + 128.0 * h), preferred_element_type=f32)
        note_ref[h : h + 1, :] = (here[0:1] - 1.0).astype(jnp.int32)
        here = jnp.dot(late_slots, ones_where(to_turn == lane + 128.0 * h), preferred_element_type=f32)
        note_ref[halves + h : halves + h + 1, :] = here[0:1].astype(jnp.int32)
    sums = jnp.where(lane[0:1] == 0.0, total, jnp.sum(late, axis=1, keepdims=True))
    for b in range(records // 64):
        here = jnp.where((slots >= 64.0 * b) & (slots < 64.0 * b + 64.0), late, 0.0)
        sums = jnp.where(lane[0:1] == 2.0 + b, jnp.sum(here, axis=1, keepdims=True), sums)
    note_ref[2 * halves : 2 * halves + 1, :] = sums.astype(jnp.int32)


def kind_of(flag):
    return 5.0 - 4.0 * flag.astype(f32)


def splat_kernel(spread_ref, rec_ref, near_ref, first_ref, second_ref, left_ref, right_ref, meta_ref, sem,
                 note_ref, slot_ref, piece_ref, turn_ref, px_ref, py_ref, pz_ref, dyz_ref, acc_ref):
    records = rec_ref.shape[0]
    halves = records // 128
    nx, ny = left_ref.shape[0], first_ref.shape[1]

    notes = rec_ref[:, 3, :]
    arrange(notes, note_ref, slot_ref)
    index = lax.broadcasted_iota(jnp.int32, (records, records), 0).astype(f32)
    to_slot = ones_where(index == slot_ref[...])
    pieces = [[], [], []]
    for c in range(3):
        whole = rec_ref[:, c, :]
        high = whole.astype(jnp.bfloat16)
        rest = whole - high.astype(f32)
        middle = rest.astype(jnp.bfloat16)
        pieces[0].append(high)
        pieces[1].append(middle)
        pieces[2].append((rest - middle.astype(f32)).astype(jnp.bfloat16))
    for n in range(3):
        for c in range(3):
            piece_ref[n * 3 + c] = jnp.dot(to_slot, pieces[n][c], preferred_element_type=f32)
    placed = jnp.dot(to_slot, notes.astype(jnp.bfloat16), preferred_element_type=f32)
    for b in range(records // 64):
        least = jnp.min(placed[b * 64 : b * 64 + 64, :], axis=0, keepdims=True)
        note_ref[2 * halves + 1 + b : 2 * halves + 2 + b, :] = least.astype(jnp.int32)
    copy = pltpu.make_async_copy(note_ref, meta_ref, sem)
    copy.start()
    near_ref[...] = jnp.full(near_ref.shape, FAR, f32)
    turn_ref[...] = jnp.zeros(turn_ref.shape, f32)
    copy.wait()
    batches = (meta_ref[2 * halves, 0] + 63) // 64
    late = meta_ref[2 * halves, 1]

    lane = lax.broadcasted_iota(jnp.int32, (8, 128), 1)
    depth = (lane & 15).astype(f32) + 0.5
    spots = lax.broadcasted_iota(jnp.int32, (1, 128), 1) >> 4

    def batch(g, carry):
        turns = []
        for s in range(8):
            for n in range(9):
                turn_ref[s, n * 8 : n * 8 + 8, :] = piece_ref[n, pl.ds(pl.multiple_of(g * 64 + s * 8, 8), 8), :]
            turns.append(jnp.transpose(turn_ref[s], (1, 0)).astype(jnp.bfloat16))
        place = jnp.dot(jnp.concatenate(turns, axis=0), spread_ref[...], preferred_element_type=f32)
        for s in range(8):
            at = slice(s * TILE, s * TILE + TILE)
            px_ref[pl.ds(s, TILE, stride=8), :] = place[at, 0:128]
            py_ref[pl.ds(s, TILE, stride=8), :] = place[at, 128:256]
            pz_ref[pl.ds(s, TILE, stride=8), :] = place[at, 256:384]

        def prepare(k, inner):
            for u in range(16):
                p = k * 16 + u
                rows = pl.ds(pl.multiple_of(p * 8, 8), 8)
                py = py_ref[rows, :]
                dz = depth - pz_ref[rows, :]
                dz = dz * dz
                for y in range(16):
                    dy = (y + 0.5) - py
                    dyz_ref[p * 16 + y] = dy * dy + dz
            return inner

        lax.fori_loop(0, TILE // 16, prepare, 0)

        for k in range(PAIRS):
            stop = -meta_ref[2 * halves + 1 + g, 1 + PAIRS + k]
            steps = (stop - (meta_ref[2 * halves + 1 + g, 1 + k] + TILE) + 7) // 8
            first = jnp.maximum(stop - steps * 8, 0)

            def step(i, accs):
                accs = list(accs)
                for u in range(4):
                    p = first + i * 8 + u * 2
                    away = []
                    for v in range(2):
                        px = px_ref[pl.ds(pl.multiple_of((p + v) * 8, 8), 8), :]
                        d0 = (2 * k + 0.5) - px
                        d1 = (2 * k + 1.5) - px
                        away.append((d0 * d0, d1 * d1))
                    for y in range(16):
                        one = dyz_ref[p * 16 + y]
                        two = dyz_ref[p * 16 + 16 + y]
                        for x in range(2):
                            both = jnp.minimum(one + away[0][x], two + away[1][x])
                            accs[x * 16 + y] = jnp.minimum(accs[x * 16 + y], both)
                return tuple(accs)

            accs = lax.fori_loop(0, steps, step, tuple(jnp.full((8, 128), FAR, f32) for _ in range(32)))
            for i in range(32):
                acc_ref[(k * 32 + i) * 8 : (k * 32 + i) * 8 + 8, :] = accs[i]

        def put_down(s, t, label, mask, move):
            bx = label // 64
            base = (label // 8 % 2) * ny + bx * (32 * ny) + label // 16 % 4 * 16
            for x in range(16):
                tile = acc_ref[pl.ds(x * 128 + s, 16, stride=8), :]
                tile = pltpu.roll(tile, move, 1)
                rows = pl.ds(pl.multiple_of(base + x * (2 * ny), 16), 16)
                near_ref[rows, :] = jnp.minimum(near_ref[rows, :], jnp.where(mask, tile, FAR))

        def merge(s, inner):
            labels = [meta_ref[g // 2, g % 2 * 64 + s * 8 + t] for t in range(8)]
            wanted = [(label >= 0) & ((label & 7) == t) for t, label in enumerate(labels)]
            masks = [spots == jnp.where(want, t, -1) for t, want in enumerate(wanted)]
            labels = [jnp.maximum(label, 0) for label in labels]
            bases = [v // 8 % 2 * ny + v // 64 * (32 * ny) + v // 16 % 4 * 16 for v in labels]
            for start in range(0, 16, 8):
                tiles = [acc_ref[pl.ds(x * 128 + s, 16, stride=8), :] for x in range(start, start + 8)]
                for mask, base in zip(masks, bases):
                    for x, tile in enumerate(tiles):
                        rows = pl.ds(pl.multiple_of(base + (start + x) * (2 * ny), 16), 16)
                        near_ref[rows, :] = jnp.minimum(near_ref[rows, :], jnp.where(mask, tile, FAR))
            return inner

        lax.fori_loop(0, 8, merge, 0, unroll=2)

        def merge_late(i, inner):
            j = meta_ref[halves + i // 128, i % 128] - 1
            here = j // 64 == g
            j = jnp.maximum(j, 0)
            t = j % 8
            label = jnp.maximum(meta_ref[j // 128, j % 128], 0)
            spot = label & 7
            put_down(j // 8 % 8, t, label, spots == jnp.where(here, spot, -1), ((spot - t) & 7) * 16)
            return inner

        steps = jnp.where(meta_ref[2 * halves, 2 + g] > 0, (late + 3) // 4, 0)

        def merge_late_four(i, inner):
            for n in range(4):
                merge_late(i * 4 + n, inner)
            return inner

        lax.fori_loop(0, steps, merge_late_four, 0)
        return carry

    lax.fori_loop(0, batches, batch, 0)

    def size_at(row, rows):
        return jnp.abs(level_of(near_ref[pl.ds(row, rows), :]))

    side = lax.axis_index("gx") % 2
    for at, out in (((1 - side) * (nx - HALO), first_ref), (side * (nx - HALO), second_ref)):
        for i in range(HALO):
            for half in range(2):
                row = pl.multiple_of((at + i) * (2 * ny) + half * ny, ny)
                out[i, :, half * 128 : half * 128 + 128] = size_at(row, ny)
    for x in range(nx):
        for half in range(2):
            lanes = slice(half * 128, half * 128 + 128)
            row = (x * 2 + half) * ny
            left_ref[x, :, lanes] = size_at(row, HALO)
            right_ref[x, :, lanes] = size_at(row + ny - HALO, HALO)


def level_of(near):
    return jnp.minimum(jnp.sqrt(near) - RADIUS, BAND)


def along(pair):
    rows = pair[0].shape[0]
    lane = lax.broadcasted_iota(jnp.int32, (rows, 128), 1)
    first = lane == 0
    last = lane == 127
    up = [pltpu.roll(v, 1, 1) for v in pair]
    down = [pltpu.roll(v, 127, 1) for v in pair]
    return (
        (jnp.where(first, 0.0, up[0]), jnp.where(last, down[1], down[0])),
        (jnp.where(first, up[0], up[1]), jnp.where(last, 0.0, down[1])),
    )


def coefficients(a_ref, u_ref, x, r0, rows):
    at = slice(r0, r0 + rows)
    mags = [a_ref[x, h, at, :] for h in range(2)]
    kinds = [u_ref[x, h, at, :] for h in range(2)]
    za, zu = along(mags), along(kinds)
    result = []
    for h in range(2):
        a, u = mags[h], kinds[h]
        r = 1.0 / jnp.maximum(a, 1e-30)
        diagonal = None
        near = [(za[h][0], zu[h][0]), (za[h][1], zu[h][1])]
        for dx, dy in ((-1, 0), (1, 0), (0, -1), (0, 1)):
            beside = slice(r0 + dy, r0 + dy + rows)
            near.append((a_ref[x + dx, h, beside, :], u_ref[x + dx, h, beside, :]))
        for b, w in near:
            term = jnp.minimum(jnp.maximum(a + b, 1.0) * r, w)
            diagonal = term if diagonal is None else diagonal + term
        result.append(jnp.where(u == 1.0, WEIGHT / jnp.maximum(diagonal, 1.0), 0.0))
    return result


def interior_kernel(near_ref, flag_in, div_in, out_ref, size_ref, kind_ref, c_ref, p_ref, a_ref, u_ref, d_ref, f_ref, sem):
    nx, _, ny, _ = near_ref.shape
    R = ROWS
    copies = []
    for half in range(2):
        lanes = pl.ds(half * 128, 128)
        copies.append(pltpu.make_async_copy(flag_in.at[:, :, lanes], f_ref.at[:, half], sem.at[0, half]))
        copies.append(pltpu.make_async_copy(div_in.at[:, :, lanes], d_ref.at[:, half], sem.at[1, half]))
    for copy in copies:
        copy.start()

    def levels(x, carry):
        for half in range(2):
            level = level_of(near_ref[x, half])
            out_ref[x, :, half * 128 : half * 128 + 128] = level
            size = jnp.abs(level)
            size_ref[x, half] = size
            a_ref[x, half, R : R + ny, :] = size
        return carry

    lax.fori_loop(0, nx, levels, 0, unroll=2)
    for copy in copies:
        copy.wait()

    def convert(x, carry):
        for half in range(2):
            kind = kind_of(f_ref[x, half])
            kind_ref[x, half] = kind
            u_ref[x, half, R : R + ny, :] = kind
        return carry

    lax.fori_loop(0, nx, convert, 0, unroll=2)

    def weigh(x, carry):
        for half, c in enumerate(coefficients(a_ref, u_ref, x, R, ny)):
            c_ref[x, half] = c
            p_ref[x, half, R : R + ny, :] = c * d_ref[x, half]
        return carry

    lax.fori_loop(1, nx - 1, weigh, 0, unroll=2)


def interior(near, flag, divergence):
    vmem, hbm, _ = specs()
    nx, ny, nz = divergence.shape
    whole = jax.ShapeDtypeStruct((nx, 2, ny, 128), f32)
    padded = (nx, 2, ny + 2 * ROWS, 128)
    return pl.pallas_call(
        interior_kernel,
        out_shape=(jax.ShapeDtypeStruct((nx, ny, nz), f32),) + (whole,) * 3 + (jax.ShapeDtypeStruct(padded, f32),),
        in_specs=[vmem, hbm, hbm],
        out_specs=(vmem,) * 5,
        scratch_shapes=[
            pltpu.VMEM(padded, f32),
            pltpu.VMEM(padded, f32),
            pltpu.VMEM(whole.shape, f32),
            pltpu.VMEM(whole.shape, jnp.int32),
            pltpu.SemaphoreType.DMA((2, 2)),
        ],
        compiler_params=pltpu.CompilerParams(vmem_limit_bytes=36 << 20),
        name="interior",
    )(near.reshape(whole.shape), flag, divergence)


def specs():
    return tuple(pl.BlockSpec(memory_space=space) for space in (pltpu.VMEM, pl.ANY, pltpu.HBM))


def pack(dest, block, pos, flag, divergence, bricks):
    vmem, _, hbm = specs()
    nx, ny, nz = divergence.shape
    strip = jax.ShapeDtypeStruct((2, HALO, ny, nz), f32)
    edge = jax.ShapeDtypeStruct((2, nx, HALO, nz), f32)
    return pl.pallas_call(
        pack_kernel,
        out_shape=(jax.ShapeDtypeStruct((bricks * 2, 4, TILE), f32), strip, strip, edge, edge),
        in_specs=[hbm] * 5,
        out_specs=(vmem,) * 5,
        scratch_shapes=[
            pltpu.SMEM(dest.shape, jnp.int32),
            pltpu.SMEM(block.shape, jnp.int32),
            pltpu.VMEM(pos.shape, f32),
            pltpu.SMEM((bricks,), jnp.int32),
            pltpu.VMEM((4, TILE, TILE), f32),
            pltpu.VMEM((4, TILE + 16, TILE), f32),
            pltpu.VMEM((2, HALO, ny, nz), jnp.int32),
            pltpu.VMEM((2, nx, 8, nz), jnp.int32),
            pltpu.VMEM((2, nx, 8, nz), f32),
            pltpu.SemaphoreType.DMA((3,)),
            pltpu.SemaphoreType.DMA((8,)),
        ],
        compiler_params=pltpu.CompilerParams(vmem_limit_bytes=60 << 20),
        name="pack",
    )(dest, block, pos, flag, divergence)


def splat(arrived, nx, ny, nz):
    vmem, _, _ = specs()
    records = arrived.shape[0]
    strip = jax.ShapeDtypeStruct((HALO, ny, nz), f32)
    edge = jax.ShapeDtypeStruct((nx, HALO, nz), f32)
    return pl.pallas_call(
        splat_kernel,
        out_shape=(
            jax.ShapeDtypeStruct((nx * 2 * ny, 128), f32),
            strip,
            strip,
            edge,
            edge,
        ),
        in_specs=[vmem, vmem],
        out_specs=(vmem,) * 5,
        scratch_shapes=[
            pltpu.SMEM((16, 128), jnp.int32),
            pltpu.SemaphoreType.DMA,
            pltpu.VMEM((16, 128), jnp.int32),
            pltpu.VMEM((1, records), f32),
            pltpu.VMEM((9, records, TILE), f32),
            pltpu.VMEM((8, 128, TILE), f32),
            pltpu.VMEM((TILE * 8 + 8, 128), f32),
            pltpu.VMEM((TILE * 8 + 8, 128), f32),
            pltpu.VMEM((TILE * 8 + 8, 128), f32),
            pltpu.VMEM((TILE * BLOCK, 8, 128), f32),
            pltpu.VMEM((BLOCK * BLOCK * 8 + 8, 128), f32),
        ],
        compiler_params=pltpu.CompilerParams(vmem_limit_bytes=28 << 20),
        name="splat",
    )(spread_matrix(), arrived)


def edges_kernel(left_ref, right_ref, lx1_ref, lx2_ref, ix1_ref, ix2_ref, out1_ref, out2_ref):
    nx, H = left_ref.shape[0:2]
    ny = lx1_ref.shape[1]
    side = lax.axis_index("gx") % 2
    even = lax.axis_index("gy") % 2 == 0
    ext = nx + 2 * H
    low = slice(0, H)
    high = slice(ny - H, ny)
    for turn, out in ((True, out1_ref), (False, out2_ref)):
        up = even if turn else jnp.logical_not(even)
        out[H : nx + H] = jnp.where(up, right_ref[...], left_ref[...])
        for at, step, one, two in (
            (0, nx + H, lx1_ref, lx2_ref),
            (ext, H, ix1_ref.at[0], ix2_ref.at[0]),
            (ext + 2 * H, H, ix1_ref.at[1], ix2_ref.at[1]),
        ):
            out[pl.ds(at + (1 - side) * step, H)] = jnp.where(up, one[:, high, :], one[:, low, :])
            out[pl.ds(at + side * step, H)] = jnp.where(up, two[:, high, :], two[:, low, :])


def edges(left, right, lx1, lx2, ix1, ix2):
    vmem, _, _ = specs()
    nx, H, nz = left.shape
    out = jax.ShapeDtypeStruct((nx + 6 * H, H, nz), f32)
    return pl.pallas_call(
        edges_kernel,
        out_shape=(out, out),
        in_specs=[vmem] * 6,
        out_specs=(vmem, vmem),
        compiler_params=pltpu.CompilerParams(vmem_limit_bytes=16 << 20),
        name="edges",
    )(left, right, lx1, lx2, ix1, ix2)


def around(ref, x, r0, rows):
    at = slice(r0, r0 + rows)
    pair = [ref[x, h, at, :] for h in range(2)]
    z = along(pair)
    totals = []
    for h in range(2):
        total = z[h][0] + z[h][1]
        total = total + (ref[x - 1, h, at, :] + ref[x + 1, h, at, :])
        total = total + (ref[x, h, r0 - 1 : r0 - 1 + rows, :] + ref[x, h, r0 + 1 : r0 + 1 + rows, :])
        totals.append(total)
    return pair, totals


def second_sweep(p_ref, c, x, r0, rows):
    own, total = around(p_ref, x, r0, rows)
    return [own[h] * (4.0 / 3.0) + c[h] * total[h] for h in range(2)]


def later_sweep(ref, p, c, x, r0, rows):
    own, total = around(ref, x, r0, rows)
    return [own[h] * (1.0 / 3.0) + p[h] + c[h] * total[h] for h in range(2)]


def middle_kernel(c_ref, p_ref, out_ref, q_ref, r_ref):
    nx, _, ny, _ = c_ref.shape
    R = ROWS
    at = slice(R, R + ny)

    def both(ref, x, rows=slice(None)):
        return [ref[x, h, rows, :] for h in range(2)]

    def second(x, carry):
        for h, v in enumerate(second_sweep(p_ref, both(c_ref, x), x, R, ny)):
            q_ref[x, h, at, :] = v
        return carry

    lax.fori_loop(2, nx - 2, second, 0, unroll=7)

    def third(x, carry):
        for h, v in enumerate(later_sweep(q_ref, both(p_ref, x, at), both(c_ref, x), x, R, ny)):
            r_ref[x, h, at, :] = v
        return carry

    lax.fori_loop(3, nx - 3, third, 0, unroll=13)

    def fourth(x, carry):
        for h, v in enumerate(later_sweep(r_ref, both(p_ref, x, at), both(c_ref, x), x, R, ny)):
            out_ref[x, :, h * 128 : h * 128 + 128] = v
        return carry

    lax.fori_loop(4, nx - 4, fourth, 0, unroll=8)


def middle(c, p):
    vmem, _, _ = specs()
    nx, _, ny, lanes = c.shape
    padded = jax.ShapeDtypeStruct(p.shape, f32)
    return pl.pallas_call(
        middle_kernel,
        out_shape=(jax.ShapeDtypeStruct((nx, ny, 2 * lanes), f32), padded, padded),
        in_specs=[vmem, vmem],
        out_specs=(vmem,) * 3,
        compiler_params=pltpu.CompilerParams(vmem_limit_bytes=24 << 20),
        name="middle",
    )(c, p)


def jacobi_kernel(result_in, size_ref, kind_ref, div_ref, c_in, p_in, q_in, r_in, lx1_ref, lx2_ref, ix1_ref, ix2_ref,
                  ly1_ref, ly2_ref, iy1_ref, iy2_ref, out_ref,
                  a_ref, u_ref, d_ref, c_ref, p_ref, q_ref, r_ref, slab_ref, tile_ref, sem, out_sem):
    nx, _, ny, _ = size_ref.shape
    H = HALO
    R = ROWS
    S = H + 1
    side = lax.axis_index("gx") % 2
    inner = pl.ds(R, ny)
    first_x, second_x = pl.ds((1 - side) * (nx + H), H), pl.ds(side * (nx + H), H)
    copies = []

    def copy(source, target, n, half):
        copies.append(pltpu.make_async_copy(source, target, sem.at[n, half]))
        copies[-1].start()

    shell = ((0, S, 0, ny), (nx - S, S, 0, ny), (S, nx - 2 * S, 0, 8), (S, nx - 2 * S, ny - 8, 8))
    for n, (x, planes, y, rows) in enumerate(shell):
        xs, ys, padded = pl.ds(x, planes), pl.ds(y, rows), pl.ds(y + R, rows)
        at = pl.ds(x + H, planes)
        copy(size_ref.at[xs, :, ys], a_ref.at[at, :, padded], n, 0)
        copy(kind_ref.at[xs, :, ys], u_ref.at[at, :, padded], n, 1)
        for half in range(2):
            copy(div_ref.at[xs, ys, pl.ds(half * 128, 128)], d_ref.at[at, half, padded], 4 + n, half)
        copy(c_in.at[xs, :, ys], c_ref.at[at, :, padded], 8 + n, 0)
        copy(p_in.at[xs, :, padded], p_ref.at[at, :, padded], 8 + n, 1)
    for half in range(2):
        lanes = pl.ds(half * 128, 128)
        for n, (source, target) in enumerate(
            (
                (ix1_ref.at[0], u_ref.at[first_x, half, inner]),
                (ix2_ref.at[0], u_ref.at[second_x, half, inner]),
                (ix1_ref.at[1], d_ref.at[first_x, half, inner]),
                (ix2_ref.at[1], d_ref.at[second_x, half, inner]),
                (lx1_ref, a_ref.at[first_x, half, inner]),
                (lx2_ref, a_ref.at[second_x, half, inner]),
            )
        ):
            copy(source.at[:, :, lanes], target, 16 + n, half)
    ready = len(copies)
    for m, (source, target) in enumerate(((q_in, q_ref), (r_in, r_ref))):
        for n, (x, planes, y, rows) in enumerate(shell):
            xs, padded, at = pl.ds(x, planes), pl.ds(y + R, rows), pl.ds(x + H, planes)
            copy(source.at[xs, :, padded], target.at[at, :, padded], 12 + n, m)
    mid = pl.ds(H, nx - 2 * H)
    copy(result_in.at[mid, pl.ds(0, 8)], tile_ref.at[0], 22, 0)
    copy(result_in.at[mid, pl.ds(ny - 8, 8)], tile_ref.at[1], 22, 1)
    for half in range(2):
        lanes = slice(half * 128, half * 128 + 128)
        for turn, rows in ((1, slice(R - H, R)), (0, slice(R + ny, R + ny + H))):
            first = lax.axis_index("gy") % 2 == turn
            a_ref[:, half, rows, :] = jnp.where(first, ly1_ref[0 : nx + 2 * H, :, lanes], ly2_ref[0 : nx + 2 * H, :, lanes])
            for n, ext in enumerate((u_ref, d_ref)):
                at = nx + 2 * H + n * 2 * H
                corner = jnp.where(first, ly1_ref[at : at + 2 * H, :, lanes], ly2_ref[at : at + 2 * H, :, lanes])
                ext[0:H, half, rows, :] = corner[0:H]
                ext[nx + H : nx + 2 * H, half, rows, :] = corner[H : 2 * H]
                ext[H : nx + H, half, rows, :] = jnp.where(first, iy1_ref[n, :, :, lanes], iy2_ref[n, :, :, lanes])
    for one in copies[:ready]:
        one.wait()

    def over_shell(first, body):
        last = nx + 2 * H - first - H

        def planes(i, carry):
            body(first + i, R - H, ny + 2 * H)
            body(last + i, R - H, ny + 2 * H)
            return carry

        def sides(x, carry):
            body(x, R - H, 8)
            body(x, R + ny - H, 8)
            return carry

        lax.fori_loop(0, H, planes, 0, unroll=4)
        lax.fori_loop(first + H, last, sides, 0, unroll=8)

    def both(ref, x, r0, rows):
        return [ref[x, h, r0 : r0 + rows, :] for h in range(2)]

    def weigh(x, r0, rows):
        at = slice(r0, r0 + rows)
        for half, c in enumerate(coefficients(a_ref, u_ref, x, r0, rows)):
            c_ref[x, half, at, :] = c
            p_ref[x, half, at, :] = c * d_ref[x, half, at, :]

    def second(x, r0, rows):
        for h, v in enumerate(second_sweep(p_ref, both(c_ref, x, r0, rows), x, r0, rows)):
            q_ref[x, h, r0 : r0 + rows, :] = v

    def third(x, r0, rows):
        for h, v in enumerate(later_sweep(q_ref, both(p_ref, x, r0, rows), both(c_ref, x, r0, rows), x, r0, rows)):
            r_ref[x, h, r0 : r0 + rows, :] = v

    over_shell(1, weigh)
    for one in copies[ready:]:
        one.wait()
    over_shell(2, second)
    over_shell(3, third)

    def last(x, r0, rows):
        return later_sweep(r_ref, both(p_ref, x, r0, rows), both(c_ref, x, r0, rows), x, r0, rows)

    def planes(i, carry):
        for n, x in enumerate((H + i, nx + i)):
            for h, v in enumerate(last(x, R, ny)):
                slab_ref[n, i, :, h * 128 : h * 128 + 128] = v
        return carry

    lax.fori_loop(0, H, planes, 0, unroll=4)
    outs = [
        pltpu.make_async_copy(slab_ref.at[n], out_ref.at[pl.ds(x, H)], out_sem.at[n]) for n, x in enumerate((0, nx - H))
    ]
    for one in outs:
        one.start()

    def sides(x, carry):
        for h, v in enumerate(last(x, R - H, 8)):
            tile_ref[0, x - 2 * H, 0:H, h * 128 : h * 128 + 128] = v[H:8]
        for h, v in enumerate(last(x, R + ny - H, 8)):
            tile_ref[1, x - 2 * H, 8 - H : 8, h * 128 : h * 128 + 128] = v[0:H]
        return carry

    lax.fori_loop(2 * H, nx, sides, 0, unroll=8)
    for n, y in enumerate((0, ny - 8)):
        outs.append(pltpu.make_async_copy(tile_ref.at[n], out_ref.at[mid, pl.ds(y, 8)], out_sem.at[2 + n]))
        outs[-1].start()
    for one in outs:
        one.wait()


def jacobi(result, parts, halo):
    vmem, hbm, _ = specs()
    nx, ny, nz = result.shape
    ext = (nx + 2 * HALO, 2, ny + 2 * ROWS, 128)
    return pl.pallas_call(
        jacobi_kernel,
        out_shape=jax.ShapeDtypeStruct((nx, ny, nz), f32),
        in_specs=[hbm] * 12 + [vmem] * 4,
        out_specs=hbm,
        input_output_aliases={0: 0},
        scratch_shapes=[pltpu.VMEM(ext, f32)] * 7
        + [
            pltpu.VMEM((2, HALO, ny, nz), f32),
            pltpu.VMEM((2, nx - 2 * HALO, 8, nz), f32),
            pltpu.SemaphoreType.DMA((23, 2)),
            pltpu.SemaphoreType.DMA((4,)),
        ],
        compiler_params=pltpu.CompilerParams(vmem_limit_bytes=32 << 20),
        name="jacobi",
    )(result, *parts, *halo)


def spread_matrix():
    row = jnp.arange(128)
    coord, tile = row // 8 % 3, row % 8
    column = jnp.arange(384)
    hit = (row[:, None] < 72) & (coord[:, None] == column[None, :] // 128)
    hit = hit & (tile[:, None] == column[None, :] % 128 // 16)
    return hit.astype(jnp.bfloat16)


def swap(axis, first, second):
    count = lax.axis_size(axis)
    arrived = []
    for part, start in ((first, 0), (second, 1)):
        pairs = []
        for i in range(start, count - 1, 2):
            pairs += [(i, i + 1), (i + 1, i)]
        arrived.append(lax.ppermute(part, axis, pairs))
    return arrived


def per_device(particle_pos, tile_dest, tile_block, fluid_flag, divergence):
    nx, ny, nz = divergence.shape
    bricks = lax.axis_size("gx") * lax.axis_size("gy")
    flag, div = fluid_flag, divergence
    send, first, second, face1, face2 = pack(tile_dest[:, 0], tile_block, particle_pos, flag, div, bricks)
    arrived = lax.all_to_all(send, ("gx", "gy"), split_axis=0, concat_axis=0, tiled=True)
    ix1, ix2 = swap("gx", first, second)
    iy1, iy2 = swap("gy", face1, face2)
    arrived, iy1, iy2 = lax.optimization_barrier((arrived, iy1, iy2))
    near, first, second, left, right = splat(arrived, nx, ny, nz)
    lx1, lx2 = swap("gx", first, second)
    level, sizes, kinds, c, p = interior(near, flag, div)
    lx1, lx2, c = lax.optimization_barrier((lx1, lx2, c))
    ly1, ly2 = swap("gy", *edges(left, right, lx1, lx2, ix1, ix2))
    result, q, r = middle(c, p)
    pressure = jacobi(result, (sizes, kinds, div, c, p, q, r), (lx1, lx2, ix1, ix2, ly1, ly2, iy1, iy2))
    return (level, pressure)


def solution(mesh):
    placed = (
        P(None, ("gx", "gy")),
        P(("gx", "gy"), None),
        P(("gx", "gy")),
        P("gx", "gy", None),
        P("gx", "gy", None),
    )
    return jax.shard_map(
        per_device,
        mesh=mesh,
        in_specs=placed,
        out_specs=(P("gx", "gy", None), P("gx", "gy", None)),
        check_vma=False,
    )
```

profile of v0, /device:TPU:11, one launch (start us, length us, event | category | flops | bytes accessed | tf_op | source)
XLA Modules:
  0.0 106.0 jit_solution(11035957239480735870)
XLA Ops:
  0.6 0.0 copy-start
  0.6 4.4 %pack.1 = (f32[256,4,128]{2,1,0:T(4,128)}, f32[2,4,64,256]{3,2,1,0:T(8,128)}, f32[2,4,64,256]{3,2,1,0:T(8,128)}, f32[2,32,4,256]{3,2,1,0:T(4,128)}, f32[2,32,4,256]{3,2,1,0:T(4,128)}) custom-call(s32[128]{0:T(128)} %bitcast.3, s32[128]{0:T(128)} %block_in.1, f32[3,16384]{1,0:T(4,128)} %pos_in.1, s32[32,64,256]{2,1,0:T(8,128)} %flag_in.1, f32[32,64,256]{2,1,0:T(8,128)} %div_ref.1), custom_call_target="tpu_custom_call" | custom-call | tf_op jit(solution)/shard_map/pack/pallas_call | solution.py:493
  5.0 11.2 %all-to-all-start = ((f32[256,4,128]{2,1,0:T(4,128)}), f32[256,4,128]{2,1,0:T(4,128)}, u32[]{:S(2)}, u32[]{:S(2)}) async-start(f32[256,4,128]{2,1,0:T(4,128)} %get-tuple-element.28), calls=%async_computation | async-start | bytes 1048576 | tf_op jit(solution)/shard_map/all_to_all | solution.py:829
  16.2 0.4 collective-permute-start
  16.7 3.1 %collective-permute-start.1 = (f32[2,32,4,256]{3,2,1,0:T(4,128)}, f32[2,32,4,256]{3,2,1,0:T(4,128)S(1)}, u32[]{:S(2)}, u32[]{:S(2)}) collective-permute-start(f32[2,32,4,256]{3,2,1,0:T(4,128)} %get-tuple-element.30), channel_id=1, source_target_pairs={{1,2},{2,1},{3,4},{4,3},{5,6},{6,5},{9,10},{10,9},{11,12},{12,11},... | collective-permute-start | bytes 786440 | tf_op jit(solution)/shard_map/ppermute | solution.py:820
  19.8 1.5 %collective-permute-start.4 = (f32[2,4,64,256]{3,2,1,0:T(8,128)}, f32[2,4,64,256]{3,2,1,0:T(8,128)S(1)}, u32[]{:S(2)}, u32[]{:S(2)}) collective-permute-start(f32[2,4,64,256]{3,2,1,0:T(8,128)} %get-tuple-element.46), channel_id=1, source_target_pairs={{0,8},{8,0},{16,24},{24,16},{32,40},{40,32},{48,56},{56,48},{64,72... | collective-permute-start | bytes 1572872 | tf_op jit(solution)/shard_map/ppermute | solution.py:820
  21.3 3.9 %collective-permute-start.5 = (f32[2,4,64,256]{3,2,1,0:T(8,128)}, f32[2,4,64,256]{3,2,1,0:T(8,128)S(1)}, u32[]{:S(2)}, u32[]{:S(2)}) collective-permute-start(f32[2,4,64,256]{3,2,1,0:T(8,128)} %get-tuple-element.47), channel_id=1, source_target_pairs={{8,16},{16,8},{24,32},{32,24},{40,48},{48,40},{56,64},{64,56},{72,... | collective-permute-start | bytes 1572872 | tf_op jit(solution)/shard_map/ppermute | solution.py:820
  25.3 0.1 and_convert_fusion.spread_ref
  25.4 0.0 collective-permute-done.iy1_ref
  25.4 1.2 %collective-permute-done.1.iy2_ref = f32[2,32,4,256]{3,2,1,0:T(4,128)S(1)} collective-permute-done((f32[2,32,4,256]{3,2,1,0:T(4,128)}, f32[2,32,4,256]{3,2,1,0:T(4,128)S(1)}, u32[]{:S(2)}, u32[]{:S(2)}) %collective-permute-start.1) | collective-permute-done | bytes 262176 | tf_op jit(solution)/shard_map/ppermute | solution.py:820
  26.6 0.0 copy-start.2
  26.6 0.7 copy-done.2
  27.3 0.0 all-to-all-done.rec_ref
  27.4 48.1 %splat.1 = (f32[4096,128]{1,0:T(8,128)S(1)}, f32[4,64,256]{2,1,0:T(8,128)S(1)}, f32[4,64,256]{2,1,0:T(8,128)S(1)}, f32[32,4,256]{2,1,0:T(4,128)S(1)}, f32[32,4,256]{2,1,0:T(4,128)S(1)}) custom-call(bf16[128,384]{1,0:T(8,128)(2,1)S(1)} %and_convert_fusion.spread_ref, f32[256,4,128]{2,1,0:T(4,128)} %all-to-all-done.rec_ref), custom_call_target="tpu_custom_call" | custom-call | tf_op jit(solution)/shard_map/splat/pallas_call | solution.py:521
  75.5 0.1 collective-permute-start.2
  75.6 1.9 %collective-permute-start.3 = (f32[4,64,256]{2,1,0:T(8,128)S(1)}, f32[4,64,256]{2,1,0:T(8,128)S(1)}, u32[]{:S(2)}, u32[]{:S(2)}) collective-permute-start(f32[4,64,256]{2,1,0:T(8,128)S(1)} %get-tuple-element.35), channel_id=1, source_target_pairs={{8,16},{16,8},{24,32},{32,24},{40,48},{48,40},{56,64},{64,56},{72,... | collective-permute-start | bytes 786440 | tf_op jit(solution)/shard_map/ppermute | solution.py:820
  77.5 0.0 copy-done
  77.5 0.0 copy-start.1
  77.5 1.6 %copy-done.1 = s32[32,64,256]{2,1,0:T(8,128)S(1)} copy-done((s32[32,64,256]{2,1,0:T(8,128)S(1)}, s32[32,64,256]{2,1,0:T(8,128)}, u32[]{:S(2)}) %copy-start.1) | copy-done | bytes 2097176
  79.1 6.4 %interior.1 = (f32[32,64,256]{2,1,0:T(8,128)}, f32[32,2,64,128]{3,2,1,0:T(8,128)S(1)}, f32[32,2,64,128]{3,2,1,0:T(8,128)S(1)}, f32[32,2,64,128]{3,2,1,0:T(8,128)S(1)}, f32[32,2,80,128]{3,2,1,0:T(8,128)S(1)}) custom-call(f32[32,2,64,128]{3,2,1,0:T(8,128)S(1)} %bitcast.2, s32[32,64,256]{2,1,0:T(8,128)S(1)} %copy-done.1, f32[32,64,256]{2,1,0:T(8,128)S(1)} %copy-done), custom_call_target="tpu_custom_call" | custom-call | tf_op jit(solution)/shard_map/interior/pallas_call | solution.py:467
  85.5 0.0 collective-permute-done.2.lx1_ref
  85.5 0.4 collective-permute-done.3.lx2_ref
  85.9 0.0 collective-permute-done.4.ix1_ref
  85.9 0.0 collective-permute-done.5.ix2_ref
  85.9 0.1 edges.1
  86.0 1.6 %collective-permute-start.6 = (f32[56,4,256]{2,1,0:T(4,128)S(1)}, f32[56,4,256]{2,1,0:T(4,128)S(1)}, u32[]{:S(2)}, u32[]{:S(2)}) collective-permute-start(f32[56,4,256]{2,1,0:T(4,128)S(1)} %get-tuple-element.50), channel_id=1, source_target_pairs={{0,1},{1,0},{2,3},{3,2},{4,5},{5,4},{6,7},{7,6},{8,9},{9,8},{10,11... | collective-permute-start | bytes 688136 | tf_op jit(solution)/shard_map/ppermute | solution.py:820
  87.6 5.9 %collective-permute-start.7 = (f32[56,4,256]{2,1,0:T(4,128)S(1)}, f32[56,4,256]{2,1,0:T(4,128)S(1)}, u32[]{:S(2)}, u32[]{:S(2)}) collective-permute-start(f32[56,4,256]{2,1,0:T(4,128)S(1)} %get-tuple-element.51), channel_id=1, source_target_pairs={{1,2},{2,1},{3,4},{4,3},{5,6},{6,5},{9,10},{10,9},{11,12},{12,11},... | collective-permute-start | bytes 688136 | tf_op jit(solution)/shard_map/ppermute | solution.py:820
  93.6 0.0 copy-start.3
  93.6 4.8 %middle.1 = (f32[32,64,256]{2,1,0:T(8,128)}, f32[32,2,80,128]{3,2,1,0:T(8,128)S(1)}, f32[32,2,80,128]{3,2,1,0:T(8,128)S(1)}) custom-call(f32[32,2,64,128]{3,2,1,0:T(8,128)S(1)} %get-tuple-element.37.c_ref.c_in, f32[32,2,80,128]{3,2,1,0:T(8,128)S(1)} %get-tuple-element.38.p_ref.p_in), custom_call_target="tpu_custom_call" | custom-call | tf_op jit(solution)/shard_map/middle/pallas_call | solution.py:641
  98.4 0.0 collective-permute-done.6.ly1_ref
  98.4 0.0 collective-permute-done.7.ly2_ref
  98.4 0.0 copy-done.3
  98.4 7.4 %jacobi.1 = f32[32,64,256]{2,1,0:T(8,128)} custom-call(f32[32,64,256]{2,1,0:T(8,128)} %get-tuple-element.39.result_in, f32[32,2,64,128]{3,2,1,0:T(8,128)S(1)} %get-tuple-element.40.size_ref, f32[32,2,64,128]{3,2,1,0:T(8,128)S(1)} %get-tuple-element.41.kind_ref, f32[32,64,256]{2,1,0:T(8,128)S(1)} %copy-done, ...), custom_call_target="tpu_custom_call", output_to_operand_aliasing={{}: (0, {})} | custom-call | tf_op jit(solution)/shard_map/jacobi/pallas_call | solution.py:786
  (3 shorter events, 0.0 us)
Async XLA Ops:
  0.6 76.9 %copy-start = (f32[32,64,256]{2,1,0:T(8,128)S(1)}, f32[32,64,256]{2,1,0:T(8,128)}, u32[]{:S(2)}) copy-start(f32[32,64,256]{2,1,0:T(8,128)} %div_ref.1) | copy-start | bytes 6291460
  5.0 22.3 %all-to-all-start = ((f32[256,4,128]{2,1,0:T(4,128)}), f32[256,4,128]{2,1,0:T(4,128)}, u32[]{:S(2)}, u32[]{:S(2)}) async-start(f32[256,4,128]{2,1,0:T(4,128)} %get-tuple-element.28), calls=%async_computation | async-start | bytes 1048576 | tf_op jit(solution)/shard_map/all_to_all | solution.py:829
  16.2 9.2 %collective-permute-start = (f32[2,32,4,256]{3,2,1,0:T(4,128)}, f32[2,32,4,256]{3,2,1,0:T(4,128)S(1)}, u32[]{:S(2)}, u32[]{:S(2)}) collective-permute-start(f32[2,32,4,256]{3,2,1,0:T(4,128)} %get-tuple-element.29), channel_id=1, source_target_pairs={{0,1},{1,0},{2,3},{3,2},{4,5},{5,4},{6,7},{7,6},{8,9},{9,8},{10,11... | collective-permute-start | bytes 786440 | tf_op jit(solution)/shard_map/ppermute | solution.py:820
  16.7 10.0 %collective-permute-start.1 = (f32[2,32,4,256]{3,2,1,0:T(4,128)}, f32[2,32,4,256]{3,2,1,0:T(4,128)S(1)}, u32[]{:S(2)}, u32[]{:S(2)}) collective-permute-start(f32[2,32,4,256]{3,2,1,0:T(4,128)} %get-tuple-element.30), channel_id=1, source_target_pairs={{1,2},{2,1},{3,4},{4,3},{5,6},{6,5},{9,10},{10,9},{11,12},{12,11},... | collective-permute-start | bytes 786440 | tf_op jit(solution)/shard_map/ppermute | solution.py:820
  19.8 66.1 %collective-permute-start.4 = (f32[2,4,64,256]{3,2,1,0:T(8,128)}, f32[2,4,64,256]{3,2,1,0:T(8,128)S(1)}, u32[]{:S(2)}, u32[]{:S(2)}) collective-permute-start(f32[2,4,64,256]{3,2,1,0:T(8,128)} %get-tuple-element.46), channel_id=1, source_target_pairs={{0,8},{8,0},{16,24},{24,16},{32,40},{40,32},{48,56},{56,48},{64,72... | collective-permute-start | bytes 1572872 | tf_op jit(solution)/shard_map/ppermute | solution.py:820
  21.3 64.6 %collective-permute-start.5 = (f32[2,4,64,256]{3,2,1,0:T(8,128)}, f32[2,4,64,256]{3,2,1,0:T(8,128)S(1)}, u32[]{:S(2)}, u32[]{:S(2)}) collective-permute-start(f32[2,4,64,256]{3,2,1,0:T(8,128)} %get-tuple-element.47), channel_id=1, source_target_pairs={{8,16},{16,8},{24,32},{32,24},{40,48},{48,40},{56,64},{64,56},{72,... | collective-permute-start | bytes 1572872 | tf_op jit(solution)/shard_map/ppermute | solution.py:820
  26.6 0.7 copy-start.2
  75.5 10.0 %collective-permute-start.2 = (f32[4,64,256]{2,1,0:T(8,128)S(1)}, f32[4,64,256]{2,1,0:T(8,128)S(1)}, u32[]{:S(2)}, u32[]{:S(2)}) collective-permute-start(f32[4,64,256]{2,1,0:T(8,128)S(1)} %get-tuple-element.34), channel_id=1, source_target_pairs={{0,8},{8,0},{16,24},{24,16},{32,40},{40,32},{48,56},{56,48},{64,72... | collective-permute-start | bytes 786440 | tf_op jit(solution)/shard_map/ppermute | solution.py:820
  75.6 10.3 %collective-permute-start.3 = (f32[4,64,256]{2,1,0:T(8,128)S(1)}, f32[4,64,256]{2,1,0:T(8,128)S(1)}, u32[]{:S(2)}, u32[]{:S(2)}) collective-permute-start(f32[4,64,256]{2,1,0:T(8,128)S(1)} %get-tuple-element.35), channel_id=1, source_target_pairs={{8,16},{16,8},{24,32},{32,24},{40,48},{48,40},{56,64},{64,56},{72,... | collective-permute-start | bytes 786440 | tf_op jit(solution)/shard_map/ppermute | solution.py:820
  77.5 1.6 %copy-start.1 = (s32[32,64,256]{2,1,0:T(8,128)S(1)}, s32[32,64,256]{2,1,0:T(8,128)}, u32[]{:S(2)}) copy-start(s32[32,64,256]{2,1,0:T(8,128)} %flag_in.1) | copy-start | bytes 6291460
  86.0 12.4 %collective-permute-start.6 = (f32[56,4,256]{2,1,0:T(4,128)S(1)}, f32[56,4,256]{2,1,0:T(4,128)S(1)}, u32[]{:S(2)}, u32[]{:S(2)}) collective-permute-start(f32[56,4,256]{2,1,0:T(4,128)S(1)} %get-tuple-element.50), channel_id=1, source_target_pairs={{0,1},{1,0},{2,3},{3,2},{4,5},{5,4},{6,7},{7,6},{8,9},{9,8},{10,11... | collective-permute-start | bytes 688136 | tf_op jit(solution)/shard_map/ppermute | solution.py:820
  87.6 10.7 %collective-permute-start.7 = (f32[56,4,256]{2,1,0:T(4,128)S(1)}, f32[56,4,256]{2,1,0:T(4,128)S(1)}, u32[]{:S(2)}, u32[]{:S(2)}) collective-permute-start(f32[56,4,256]{2,1,0:T(4,128)S(1)} %get-tuple-element.51), channel_id=1, source_target_pairs={{1,2},{2,1},{3,4},{4,3},{5,6},{6,5},{9,10},{10,9},{11,12},{12,11},... | collective-permute-start | bytes 688136 | tf_op jit(solution)/shard_map/ppermute | solution.py:820
  93.6 4.8 %copy-start.3 = (f32[2,32,4,256]{3,2,1,0:T(4,128)S(1)}, f32[2,32,4,256]{3,2,1,0:T(4,128)}, u32[]{:S(2)}) copy-start(f32[2,32,4,256]{3,2,1,0:T(4,128)} %copy-done.2) | copy-start | bytes 786436
where the time goes:
time: 106 us
  Pallas kernels  71.2 us (67%)
  starting transfers between devices  29.8 us (28%)
  local copies, waits for them, and re-layouts  2.3 us (2%)
  waiting for transfers between devices  1.65 us (2%)
    pallas_call x1, Pallas kernels, splat(): pl.pallas_call(splat_kernel, out_shape=(jax.ShapeDtypeStruct((nx * 2 * ny...  48.1 us
    ppermute x8, starting transfers between devices, swap(): arrived.append(lax.ppermute(part, axis, pairs))  18.6 us
    all_to_all x1, starting transfers between devices, per_device(): lax.all_to_all(send, ('gx', 'gy'), split_axis=0, concat_axis=0, tiled=True)  11.2 us
    pallas_call x1, Pallas kernels, jacobi(): pl.pallas_call(jacobi_kernel, out_shape=jax.ShapeDtypeStruct((nx, ny, nz)...  7.45 us
    pallas_call x1, Pallas kernels, interior(): pl.pallas_call(interior_kernel, out_shape=(jax.ShapeDtypeStruct((nx, ny,...  6.36 us
    pallas_call x1, Pallas kernels, middle(): pl.pallas_call(middle_kernel, out_shape=(jax.ShapeDtypeStruct((nx, ny, 2...  4.79 us
    pallas_call x1, Pallas kernels, pack(): pl.pallas_call(pack_kernel, out_shape=(jax.ShapeDtypeStruct((bricks * 2,...  4.38 us
    unnamed x8, local copies, waits for them, and re-layouts  2.3 us
  transfers between devices with their start and end apart: 9, of which 2 were waited for; matrix products, arithmetic and copies ran while one was open for 0% of the time, Pallas kernels for 56%

commit v1 on v0

--- a/solution.py
+++ b/solution.py
@@ -338,7 +338,7 @@
                         near_ref[rows, :] = jnp.minimum(near_ref[rows, :], jnp.where(mask, tile, FAR))
             return inner
 
-        lax.fori_loop(0, 8, merge, 0, unroll=2)
+        lax.fori_loop(0, 8, merge, 0, unroll=4)
 
         def merge_late(i, inner):
             j = meta_ref[halves + i // 128, i % 128] - 1

time: 106 us -> 106 us (level)
  the two profiles are of different devices: /device:TPU:11 before, /device:TPU:13 now
where the time goes in v1:
time: 106 us; the launch traced here: 105 us
  starting transfers between devices  51.8 us (49%)
  Pallas kernels  49.2 us (46%)
  local copies, waits for them, and re-layouts  2.3 us (2%)
    ppermute x8, starting transfers between devices, swap(): arrived.append(lax.ppermute(part, axis, pairs))  40.6 us
    pallas_call x1, Pallas kernels, splat(): pl.pallas_call(splat_kernel, out_shape=(jax.ShapeDtypeStruct((nx * 2 * ny...  26.2 us
    all_to_all x1, starting transfers between devices, per_device(): lax.all_to_all(send, ('gx', 'gy'), split_axis=0, concat_axis=0, tiled=True)  11.2 us
    pallas_call x1, Pallas kernels, jacobi(): pl.pallas_call(jacobi_kernel, out_shape=jax.ShapeDtypeStruct((nx, ny, nz)...  7.45 us
    pallas_call x1, Pallas kernels, interior(): pl.pallas_call(interior_kernel, out_shape=(jax.ShapeDtypeStruct((nx, ny,...  6.36 us
    pallas_call x1, Pallas kernels, middle(): pl.pallas_call(middle_kernel, out_shape=(jax.ShapeDtypeStruct((nx, ny, 2...  4.79 us
    pallas_call x1, Pallas kernels, pack(): pl.pallas_call(pack_kernel, out_shape=(jax.ShapeDtypeStruct((bricks * 2,...  4.38 us
    unnamed x8, local copies, waits for them, and re-layouts  2.3 us
  transfers between devices with their start and end apart: 9, of which 1 were waited for; matrix products, arithmetic and copies ran while one was open for 0% of the time, Pallas kernels for 35%

profile of v1, /device:TPU:13, one launch (start us, length us, event | category | flops | bytes accessed | tf_op | source)
XLA Modules:
  0.0 105.4 jit_solution(18255675701150966369)
XLA Ops:
  0.6 0.0 copy-start
  0.6 4.4 %pack.1 = (f32[256,4,128]{2,1,0:T(4,128)}, f32[2,4,64,256]{3,2,1,0:T(8,128)}, f32[2,4,64,256]{3,2,1,0:T(8,128)}, f32[2,32,4,256]{3,2,1,0:T(4,128)}, f32[2,32,4,256]{3,2,1,0:T(4,128)}) custom-call(s32[128]{0:T(128)} %bitcast.3, s32[128]{0:T(128)} %block_in.1, f32[3,16384]{1,0:T(4,128)} %pos_in.1, s32[32,64,256]{2,1,0:T(8,128)} %flag_in.1, f32[32,64,256]{2,1,0:T(8,128)} %div_ref.1), custom_call_target="tpu_custom_call" | custom-call | tf_op jit(solution)/shard_map/pack/pallas_call | solution.py:493
  5.0 11.2 %all-to-all-start = ((f32[256,4,128]{2,1,0:T(4,128)}), f32[256,4,128]{2,1,0:T(4,128)}, u32[]{:S(2)}, u32[]{:S(2)}) async-start(f32[256,4,128]{2,1,0:T(4,128)} %get-tuple-element.28), calls=%async_computation | async-start | bytes 1048576 | tf_op jit(solution)/shard_map/all_to_all | solution.py:829
  16.2 0.4 collective-permute-start
  16.6 3.1 %collective-permute-start.1 = (f32[2,32,4,256]{3,2,1,0:T(4,128)}, f32[2,32,4,256]{3,2,1,0:T(4,128)S(1)}, u32[]{:S(2)}, u32[]{:S(2)}) collective-permute-start(f32[2,32,4,256]{3,2,1,0:T(4,128)} %get-tuple-element.30), channel_id=1, source_target_pairs={{1,2},{2,1},{3,4},{4,3},{5,6},{6,5},{9,10},{10,9},{11,12},{12,11},... | collective-permute-start | bytes 786440 | tf_op jit(solution)/shard_map/ppermute | solution.py:820
  19.8 1.5 %collective-permute-start.4 = (f32[2,4,64,256]{3,2,1,0:T(8,128)}, f32[2,4,64,256]{3,2,1,0:T(8,128)S(1)}, u32[]{:S(2)}, u32[]{:S(2)}) collective-permute-start(f32[2,4,64,256]{3,2,1,0:T(8,128)} %get-tuple-element.46), channel_id=1, source_target_pairs={{0,8},{8,0},{16,24},{24,16},{32,40},{40,32},{48,56},{56,48},{64,72... | collective-permute-start | bytes 1572872 | tf_op jit(solution)/shard_map/ppermute | solution.py:820
  21.3 3.9 %collective-permute-start.5 = (f32[2,4,64,256]{3,2,1,0:T(8,128)}, f32[2,4,64,256]{3,2,1,0:T(8,128)S(1)}, u32[]{:S(2)}, u32[]{:S(2)}) collective-permute-start(f32[2,4,64,256]{3,2,1,0:T(8,128)} %get-tuple-element.47), channel_id=1, source_target_pairs={{8,16},{16,8},{24,32},{32,24},{40,48},{48,40},{56,64},{64,56},{72,... | collective-permute-start | bytes 1572872 | tf_op jit(solution)/shard_map/ppermute | solution.py:820
  25.3 0.1 and_convert_fusion.spread_ref
  25.4 0.0 collective-permute-done.iy1_ref
  25.4 1.0 collective-permute-done.1.iy2_ref
  26.4 0.0 copy-start.2
  26.4 0.7 copy-done.2
  27.1 0.0 all-to-all-done.rec_ref
  27.1 26.2 %splat.1 = (f32[4096,128]{1,0:T(8,128)S(1)}, f32[4,64,256]{2,1,0:T(8,128)S(1)}, f32[4,64,256]{2,1,0:T(8,128)S(1)}, f32[32,4,256]{2,1,0:T(4,128)S(1)}, f32[32,4,256]{2,1,0:T(4,128)S(1)}) custom-call(bf16[128,384]{1,0:T(8,128)(2,1)S(1)} %and_convert_fusion.spread_ref, f32[256,4,128]{2,1,0:T(4,128)} %all-to-all-done.rec_ref), custom_call_target="tpu_custom_call" | custom-call | tf_op jit(solution)/shard_map/splat/pallas_call | solution.py:521
  53.3 21.1 %collective-permute-start.2 = (f32[4,64,256]{2,1,0:T(8,128)S(1)}, f32[4,64,256]{2,1,0:T(8,128)S(1)}, u32[]{:S(2)}, u32[]{:S(2)}) collective-permute-start(f32[4,64,256]{2,1,0:T(8,128)S(1)} %get-tuple-element.34), channel_id=1, source_target_pairs={{0,8},{8,0},{16,24},{24,16},{32,40},{40,32},{48,56},{56,48},{64,72... | collective-permute-start | bytes 786440 | tf_op jit(solution)/shard_map/ppermute | solution.py:820
  74.3 7.8 %collective-permute-start.3 = (f32[4,64,256]{2,1,0:T(8,128)S(1)}, f32[4,64,256]{2,1,0:T(8,128)S(1)}, u32[]{:S(2)}, u32[]{:S(2)}) collective-permute-start(f32[4,64,256]{2,1,0:T(8,128)S(1)} %get-tuple-element.35), channel_id=1, source_target_pairs={{8,16},{16,8},{24,32},{32,24},{40,48},{48,40},{56,64},{64,56},{72,... | collective-permute-start | bytes 786440 | tf_op jit(solution)/shard_map/ppermute | solution.py:820
  82.2 0.0 copy-done
  82.2 0.0 copy-start.1
  82.2 1.6 %copy-done.1 = s32[32,64,256]{2,1,0:T(8,128)S(1)} copy-done((s32[32,64,256]{2,1,0:T(8,128)S(1)}, s32[32,64,256]{2,1,0:T(8,128)}, u32[]{:S(2)}) %copy-start.1) | copy-done | bytes 2097176
  83.8 6.4 %interior.1 = (f32[32,64,256]{2,1,0:T(8,128)}, f32[32,2,64,128]{3,2,1,0:T(8,128)S(1)}, f32[32,2,64,128]{3,2,1,0:T(8,128)S(1)}, f32[32,2,64,128]{3,2,1,0:T(8,128)S(1)}, f32[32,2,80,128]{3,2,1,0:T(8,128)S(1)}) custom-call(f32[32,2,64,128]{3,2,1,0:T(8,128)S(1)} %bitcast.2, s32[32,64,256]{2,1,0:T(8,128)S(1)} %copy-done.1, f32[32,64,256]{2,1,0:T(8,128)S(1)} %copy-done), custom_call_target="tpu_custom_call" | custom-call | tf_op jit(solution)/shard_map/interior/pallas_call | solution.py:467
  90.2 0.0 collective-permute-done.2.lx1_ref
  90.2 0.0 collective-permute-done.3.lx2_ref
  90.2 0.0 collective-permute-done.4.ix1_ref
  90.2 0.0 collective-permute-done.5.ix2_ref
  90.2 0.1 edges.1
  90.3 0.1 collective-permute-start.6
  90.4 2.6 %collective-permute-start.7 = (f32[56,4,256]{2,1,0:T(4,128)S(1)}, f32[56,4,256]{2,1,0:T(4,128)S(1)}, u32[]{:S(2)}, u32[]{:S(2)}) collective-permute-start(f32[56,4,256]{2,1,0:T(4,128)S(1)} %get-tuple-element.51), channel_id=1, source_target_pairs={{1,2},{2,1},{3,4},{4,3},{5,6},{6,5},{9,10},{10,9},{11,12},{12,11},... | collective-permute-start | bytes 688136 | tf_op jit(solution)/shard_map/ppermute | solution.py:820
  93.0 0.0 copy-start.3
  93.0 4.8 %middle.1 = (f32[32,64,256]{2,1,0:T(8,128)}, f32[32,2,80,128]{3,2,1,0:T(8,128)S(1)}, f32[32,2,80,128]{3,2,1,0:T(8,128)S(1)}) custom-call(f32[32,2,64,128]{3,2,1,0:T(8,128)S(1)} %get-tuple-element.37.c_ref.c_in, f32[32,2,80,128]{3,2,1,0:T(8,128)S(1)} %get-tuple-element.38.p_ref.p_in), custom_call_target="tpu_custom_call" | custom-call | tf_op jit(solution)/shard_map/middle/pallas_call | solution.py:641
  97.8 0.0 collective-permute-done.6.ly1_ref
  97.8 0.0 collective-permute-done.7.ly2_ref
  97.8 0.0 copy-done.3
  97.8 7.4 %jacobi.1 = f32[32,64,256]{2,1,0:T(8,128)} custom-call(f32[32,64,256]{2,1,0:T(8,128)} %get-tuple-element.39.result_in, f32[32,2,64,128]{3,2,1,0:T(8,128)S(1)} %get-tuple-element.40.size_ref, f32[32,2,64,128]{3,2,1,0:T(8,128)S(1)} %get-tuple-element.41.kind_ref, f32[32,64,256]{2,1,0:T(8,128)S(1)} %copy-done, ...), custom_call_target="tpu_custom_call", output_to_operand_aliasing={{}: (0, {})} | custom-call | tf_op jit(solution)/shard_map/jacobi/pallas_call | solution.py:786
  (3 shorter events, 0.0 us)
Async XLA Ops:
  0.6 81.5 %copy-start = (f32[32,64,256]{2,1,0:T(8,128)S(1)}, f32[32,64,256]{2,1,0:T(8,128)}, u32[]{:S(2)}) copy-start(f32[32,64,256]{2,1,0:T(8,128)} %div_ref.1) | copy-start | bytes 6291460
  5.0 22.1 %all-to-all-start = ((f32[256,4,128]{2,1,0:T(4,128)}), f32[256,4,128]{2,1,0:T(4,128)}, u32[]{:S(2)}, u32[]{:S(2)}) async-start(f32[256,4,128]{2,1,0:T(4,128)} %get-tuple-element.28), calls=%async_computation | async-start | bytes 1048576 | tf_op jit(solution)/shard_map/all_to_all | solution.py:829
  16.2 9.2 %collective-permute-start = (f32[2,32,4,256]{3,2,1,0:T(4,128)}, f32[2,32,4,256]{3,2,1,0:T(4,128)S(1)}, u32[]{:S(2)}, u32[]{:S(2)}) collective-permute-start(f32[2,32,4,256]{3,2,1,0:T(4,128)} %get-tuple-element.29), channel_id=1, source_target_pairs={{0,1},{1,0},{2,3},{3,2},{4,5},{5,4},{6,7},{7,6},{8,9},{9,8},{10,11... | collective-permute-start | bytes 786440 | tf_op jit(solution)/shard_map/ppermute | solution.py:820
  16.6 9.8 %collective-permute-start.1 = (f32[2,32,4,256]{3,2,1,0:T(4,128)}, f32[2,32,4,256]{3,2,1,0:T(4,128)S(1)}, u32[]{:S(2)}, u32[]{:S(2)}) collective-permute-start(f32[2,32,4,256]{3,2,1,0:T(4,128)} %get-tuple-element.30), channel_id=1, source_target_pairs={{1,2},{2,1},{3,4},{4,3},{5,6},{6,5},{9,10},{10,9},{11,12},{12,11},... | collective-permute-start | bytes 786440 | tf_op jit(solution)/shard_map/ppermute | solution.py:820
  19.8 70.4 %collective-permute-start.4 = (f32[2,4,64,256]{3,2,1,0:T(8,128)}, f32[2,4,64,256]{3,2,1,0:T(8,128)S(1)}, u32[]{:S(2)}, u32[]{:S(2)}) collective-permute-start(f32[2,4,64,256]{3,2,1,0:T(8,128)} %get-tuple-element.46), channel_id=1, source_target_pairs={{0,8},{8,0},{16,24},{24,16},{32,40},{40,32},{48,56},{56,48},{64,72... | collective-permute-start | bytes 1572872 | tf_op jit(solution)/shard_map/ppermute | solution.py:820
  21.3 68.9 %collective-permute-start.5 = (f32[2,4,64,256]{3,2,1,0:T(8,128)}, f32[2,4,64,256]{3,2,1,0:T(8,128)S(1)}, u32[]{:S(2)}, u32[]{:S(2)}) collective-permute-start(f32[2,4,64,256]{3,2,1,0:T(8,128)} %get-tuple-element.47), channel_id=1, source_target_pairs={{8,16},{16,8},{24,32},{32,24},{40,48},{48,40},{56,64},{64,56},{72,... | collective-permute-start | bytes 1572872 | tf_op jit(solution)/shard_map/ppermute | solution.py:820
  26.4 0.7 copy-start.2
  53.3 36.9 %collective-permute-start.2 = (f32[4,64,256]{2,1,0:T(8,128)S(1)}, f32[4,64,256]{2,1,0:T(8,128)S(1)}, u32[]{:S(2)}, u32[]{:S(2)}) collective-permute-start(f32[4,64,256]{2,1,0:T(8,128)S(1)} %get-tuple-element.34), channel_id=1, source_target_pairs={{0,8},{8,0},{16,24},{24,16},{32,40},{40,32},{48,56},{56,48},{64,72... | collective-permute-start | bytes 786440 | tf_op jit(solution)/shard_map/ppermute | solution.py:820
  74.3 15.8 %collective-permute-start.3 = (f32[4,64,256]{2,1,0:T(8,128)S(1)}, f32[4,64,256]{2,1,0:T(8,128)S(1)}, u32[]{:S(2)}, u32[]{:S(2)}) collective-permute-start(f32[4,64,256]{2,1,0:T(8,128)S(1)} %get-tuple-element.35), channel_id=1, source_target_pairs={{8,16},{16,8},{24,32},{32,24},{40,48},{48,40},{56,64},{64,56},{72,... | collective-permute-start | bytes 786440 | tf_op jit(solution)/shard_map/ppermute | solution.py:820
  82.2 1.6 %copy-start.1 = (s32[32,64,256]{2,1,0:T(8,128)S(1)}, s32[32,64,256]{2,1,0:T(8,128)}, u32[]{:S(2)}) copy-start(s32[32,64,256]{2,1,0:T(8,128)} %flag_in.1) | copy-start | bytes 6291460
  90.3 7.5 %collective-permute-start.6 = (f32[56,4,256]{2,1,0:T(4,128)S(1)}, f32[56,4,256]{2,1,0:T(4,128)S(1)}, u32[]{:S(2)}, u32[]{:S(2)}) collective-permute-start(f32[56,4,256]{2,1,0:T(4,128)S(1)} %get-tuple-element.50), channel_id=1, source_target_pairs={{0,1},{1,0},{2,3},{3,2},{4,5},{5,4},{6,7},{7,6},{8,9},{9,8},{10,11... | collective-permute-start | bytes 688136 | tf_op jit(solution)/shard_map/ppermute | solution.py:820
  90.4 7.4 %collective-permute-start.7 = (f32[56,4,256]{2,1,0:T(4,128)S(1)}, f32[56,4,256]{2,1,0:T(4,128)S(1)}, u32[]{:S(2)}, u32[]{:S(2)}) collective-permute-start(f32[56,4,256]{2,1,0:T(4,128)S(1)} %get-tuple-element.51), channel_id=1, source_target_pairs={{1,2},{2,1},{3,4},{4,3},{5,6},{6,5},{9,10},{10,9},{11,12},{12,11},... | collective-permute-start | bytes 688136 | tf_op jit(solution)/shard_map/ppermute | solution.py:820
  93.0 4.8 %copy-start.3 = (f32[2,32,4,256]{3,2,1,0:T(4,128)S(1)}, f32[2,32,4,256]{3,2,1,0:T(4,128)}, u32[]{:S(2)}) copy-start(f32[2,32,4,256]{3,2,1,0:T(4,128)} %copy-done.2) | copy-start | bytes 786436
